TPU v7x, 32 devices: a whole 2x2x4 slice. The times are simulated.
32 devices in a mesh: tiles: 2 (over y), rows: 4 (over z), rep: 2 (over x), sub: 2 (over core).
Axes of the slice: x: 2, y: 2, z: 4, core: 2. Of those that a mesh axis runs over, the one named last changes fastest.
Arguments:
- features: float32 [1024, 256], P(('tiles', 'rows')), parts along dimension 0, may hold values from -6 to 6
- center_weight: bfloat16 [256, 256], replicated, may hold values from -0.375 to 0.375
- neighbor_weight: bfloat16 [256, 256], replicated, may hold values from -0.375 to 0.375
- cotangent: float32 [1024, 256], P(('tiles', 'rows')), parts along dimension 0, may hold values from -6 to 6
- tile_rows: int32 [128], P(('tiles', 'rows', 'rep', 'sub')), parts along dimension 0, may hold values from 0 to 7, as said below
- tile_cols: int32 [128], P(('tiles', 'rows', 'rep', 'sub')), parts along dimension 0, may hold values from 0 to 7, as said below
- tile_links: int32 [128, 64, 64], P(('tiles', 'rows', 'rep', 'sub')), parts along dimension 0, may hold values from 0 to 1, as said below
Outputs:
- edge_out: float32 [1024, 256], P(('tiles', 'rows')), parts along dimension 0
- feature_grad: float32 [1024, 256], P(('tiles', 'rows')), parts along dimension 0
- center_grad: float32 [512, 256], P('tiles'), parts along dimension 0
- neighbor_grad: float32 [512, 256], P('tiles'), parts along dimension 0
There are 2 independent parts, one for each index of `tiles`. A program takes and returns all parts, laid end to end along the dimension named above; an argument that names none is the same for every part. Nothing has to cross between parts.
Inputs may be any that keep to these rules, and one draw needn't show every extreme that they name: `tile_rows`: the device at index r of rows, c of rep and s of sub holds 4 tiles; its tile u * 2 + q (u below 2, q below 2) lies in a block row owned by r (blocks r * 2 to r * 2 + 1). `tile_cols`: tile u * 2 + q of the device at index c of rep has its block column owned by the row index u * (size of rep) + c. `tile_links`: 0 or 1. A is symmetric tile by tile: if tile q of section u on the device (r, c, s) joins block a (of owner r) to block b (of owner k), then tile q of section r div (size of rep) on the device (k, r mod (size of rep), s) joins b to a with the transposed links. A tile whose links are all zero is an empty slot.
All inputs are finite; a program needn't handle non-finite values.
Results may differ from a plain program's by a relative error of at most 0.0059.
Values may be sent and summed in bfloat16 or wider, within the bound.
A program may use at most 64 MiB of HBM per device.

v0:
```python
import jax
import jax.numpy as jnp
from jax import lax
from jax.sharding import PartitionSpec as P


def spread(value, axis, source):
    kept = jnp.where(lax.axis_index(axis) == source, value, 0).astype(value.dtype)
    return lax.psum(kept, axis)


def passed_along(x, axis, by):
    length = lax.axis_size(axis)
    return lax.ppermute(x, axis, [(i, (i + by) % length) for i in range(length)])


def silu_slope(argument):
    sigmoid_value = jax.nn.sigmoid(argument)
    return sigmoid_value * (1.0 + argument * (1.0 - sigmoid_value))


def edge_total(center_rows, neighbor_rows, link_tile):
    pre_act = center_rows[:, None, :] + neighbor_rows[None, :, :]
    return (jnp.sum(link_tile[:, :, None] * jax.nn.silu(pre_act), axis=1),)


def edge_slopes(center_rows, neighbor_rows, scale_rows, link_tile):
    pre_act = center_rows[:, None, :] + neighbor_rows[None, :, :]
    return link_tile[:, :, None] * scale_rows[:, None, :] * silu_slope(pre_act)


def edge_gradients(center_rows, neighbor_rows, scale_rows, link_tile):
    slopes = edge_slopes(center_rows, neighbor_rows, scale_rows, link_tile)
    return (jnp.sum(slopes, axis=1), jnp.sum(slopes, axis=0))


def pick_blocks(block_pick, source, block_count):
    shaped = source.reshape(block_count, -1, source.shape[1])
    return jnp.einsum("tn,nbf->tbf", block_pick, shaped, preferred_element_type=jnp.float32)


def place_blocks(block_pick, tile_values):
    return jnp.einsum(
        "tn,tbf->nbf", block_pick.astype(jnp.float32), tile_values, precision=lax.Precision.HIGHEST
    )


def tile_loop(kernel, tile_flags, members):

    def visit(element):
        flag, operands = element
        return kernel(*operands)

    return lax.map(visit, (tile_flags, members))


def body(features, center_weight, neighbor_weight, cotangent, tile_rows, tile_cols, tile_links):
    rep_count = lax.axis_size("rep")
    row_count = lax.axis_size("rows")
    sections = row_count // rep_count
    row_index = lax.axis_index("rows")
    replica = lax.axis_index("rep")
    points, feat_width = features.shape
    block_size = tile_links.shape[1]
    block_count = points // block_size
    pair_slots = tile_rows.shape[0] // sections
    feature_half = features.astype(jnp.bfloat16)
    center = jnp.dot(feature_half, center_weight, preferred_element_type=jnp.float32).astype(
        jnp.bfloat16
    )
    neighbor = jnp.dot(feature_half, neighbor_weight, preferred_element_type=jnp.float32).astype(
        jnp.bfloat16
    )
    block_ids = jnp.arange(block_count, dtype=jnp.int32)
    row_pick = ((tile_rows - row_index * block_count)[:, None] == block_ids[None, :]).astype(
        jnp.bfloat16
    )
    col_pick = ((tile_cols % block_count)[:, None] == block_ids[None, :]).astype(jnp.bfloat16)
    link_tiles = tile_links.astype(jnp.float32)
    live_flags = jnp.max(tile_links, axis=(1, 2)) > 0
    counts = place_blocks(row_pick, jnp.sum(link_tiles, axis=2)[:, :, None]).reshape(points)

    def sectioned(array):
        return array.reshape((sections, pair_slots) + array.shape[1:])

    section_ids = jnp.arange(sections, dtype=jnp.int32)
    center_tiles = sectioned(pick_blocks(row_pick, center, block_count))
    rows_sectioned = sectioned(row_pick)
    cols_sectioned = sectioned(col_pick)
    links_sectioned = sectioned(link_tiles)
    flags_sectioned = sectioned(live_flags)

    def forward_section(running, element):
        section_id, col_picks, row_picks, link_group, tile_flags, center_group = element
        remote = spread(neighbor, "rows", section_id * rep_count + replica)
        neighbor_group = pick_blocks(col_picks, remote, block_count)
        (tile_sums,) = tile_loop(edge_total, tile_flags, (center_group, neighbor_group, link_group))
        return (running + place_blocks(row_picks, tile_sums), remote)

    start = jnp.zeros((block_count, block_size, feat_width), jnp.float32)
    running, panels = lax.scan(
        forward_section,
        start,
        (
            section_ids,
            cols_sectioned,
            rows_sectioned,
            links_sectioned,
            flags_sectioned,
            center_tiles,
        ),
    )
    edge_sums, count_sums = lax.psum((running.reshape(points, feat_width), counts), ("rep", "sub"))
    degree = count_sums + 1.0
    center_full = center.astype(jnp.float32)
    neighbor_full = neighbor.astype(jnp.float32)
    self_pre = center_full + neighbor_full
    edge_out = (edge_sums + jax.nn.silu(self_pre)) / degree[:, None]
    scaled = (cotangent / degree[:, None]).astype(jnp.bfloat16)
    scale_tiles = sectioned(pick_blocks(row_pick, scaled, block_count))

    def backward_section(center_run, element):
        col_picks, row_picks, link_group, tile_flags, center_group, scale_group, remote = element
        neighbor_group = pick_blocks(col_picks, remote, block_count)
        near_part, far_part = tile_loop(
            edge_gradients, tile_flags, (center_group, neighbor_group, scale_group, link_group)
        )
        center_run = center_run + place_blocks(row_picks, near_part)
        return (center_run, place_blocks(col_picks, far_part).reshape(points, feat_width))

    center_run, outgoing = lax.scan(
        backward_section,
        start,
        (
            cols_sectioned,
            rows_sectioned,
            links_sectioned,
            flags_sectioned,
            center_tiles,
            scale_tiles,
            panels,
        ),
    )
    center_part = center_run.reshape(points, feat_width)

    def contribution(target):
        chosen = lax.dynamic_index_in_dim(outgoing, target // rep_count, 0, keepdims=False)
        return jnp.where(target % rep_count == replica, chosen, 0.0)

    def relay_turn(turn_id, carried):
        arrived = passed_along(carried, "rows", 1)
        return arrived + contribution((row_index + row_count - 1 - turn_id) % row_count)

    neighbor_part = lax.fori_loop(
        1, row_count, relay_turn, contribution((row_index + row_count - 1) % row_count)
    )
    self_slope = scaled.astype(jnp.float32) * silu_slope(self_pre)
    center_sum, neighbor_sum = lax.psum((center_part, neighbor_part), ("rep", "sub"))
    center_half = (center_sum + self_slope).astype(jnp.bfloat16)
    neighbor_half = (neighbor_sum + self_slope).astype(jnp.bfloat16)
    feature_grad = jnp.einsum(
        "pg,fg->pf", center_half, center_weight, preferred_element_type=jnp.float32
    ) + jnp.einsum("pg,fg->pf", neighbor_half, neighbor_weight, preferred_element_type=jnp.float32)
    center_local = jnp.einsum(
        "pf,pg->fg", feature_half, center_half, preferred_element_type=jnp.float32
    )
    neighbor_local = jnp.einsum(
        "pf,pg->fg", feature_half, neighbor_half, preferred_element_type=jnp.float32
    )
    center_grad, neighbor_grad = lax.psum((center_local, neighbor_local), "rows")
    return (edge_out, feature_grad, center_grad, neighbor_grad)


def solution(mesh):
    in_specs = (
        P(("tiles", "rows"), None),
        P(),
        P(),
        P(("tiles", "rows"), None),
        P(("tiles", "rows", "rep", "sub")),
        P(("tiles", "rows", "rep", "sub")),
        P(("tiles", "rows", "rep", "sub"), None, None),
    )
    out_specs = (
        P(("tiles", "rows"), None),
        P(("tiles", "rows"), None),
        P("tiles", None),
        P("tiles", None),
    )
    return jax.shard_map(body, mesh=mesh, in_specs=in_specs, out_specs=out_specs, check_vma=False)
```

profile of v0, /device:TPU:11, one launch (start us, length us, event | category | flops | bytes accessed | tf_op | source)
XLA Modules:
  0.0 232.7 jit_solution(2121379475789620692)
XLA Ops:
  11.0 88.7 %while.86 = (s32[]{:T(128)}, f32[2,64,256]{2,0,1:T(2,128)S(1)}, bf16[2,128,256]{2,1,0:T(8,128)(2,1)S(1)}, bf16[2,2,2]{2,1,0:T(2,128)(2,1)S(1)}, f32[2,2,64,256]{...) while((s32[]{:T(128)}, f32[2,64,256]{2,0,1:T(2,128)S(1)}, ...), condition=%wide.region_5.6_spmd.clone.clone, body=%wide.region_0.5_spmd.clone.sunk.clone | while | flops 8372235 | bytes 2737650 | solution.py:101
  13.1 34.9 %all-reduce.10.cloned.1.call-done = bf16[128,256]{1,0:T(8,128)(2,1)} async-done(((bf16[128,256]{1,0:T(8,128)(2,1)}), bf16[128,256]{1,0:T(8,128)(2,1)}) %all-reduce.10.cloned.1.call-update) | async-done | bytes 65552 | tf_op jit(solution)/shard_map/while/body/eval_jaxpr/psum | solution.py:9
  49.0 5.2 %while.85 = (s32[]{:T(128)}, f32[2,64,256]{2,0,1:T(2,128)S(1)}, f32[2,64,64]{2,1,0:T(8,128)S(1)}, f32[2,64,256]{2,1,0:T(8,128)S(1)}, f32[2,64,256]{2,0,1:T(2,128)S(1)}, /*index=5*/s32[]{:T(128)}, s32[]{:T(128)}) while((s32[]{:T(128)}, f32[2,64,256]{2,0,1:T(2,128)S(1)}, f32[2,64,64]{2,1,0:T(8,128)S(1)}, f32[2,64,256]{2,1,0:T(8,128)S(1)}, ...), condition=%wide.region_4.4_spmd, body=%wide.region_2.3_spmd.sunk | while | flops 7323650 | bytes 901221 | solution.py:54
  49.1 1.5 fusion.80
  51.7 1.5 fusion.80
  57.1 35.5 %all-reduce.10.cloned.1.call-done = bf16[128,256]{1,0:T(8,128)(2,1)} async-done(((bf16[128,256]{1,0:T(8,128)(2,1)}), bf16[128,256]{1,0:T(8,128)(2,1)}) %all-reduce.10.cloned.1.call-update) | async-done | bytes 65552 | tf_op jit(solution)/shard_map/while/body/eval_jaxpr/psum | solution.py:9
  93.6 5.2 %while.85 = (s32[]{:T(128)}, f32[2,64,256]{2,0,1:T(2,128)S(1)}, f32[2,64,64]{2,1,0:T(8,128)S(1)}, f32[2,64,256]{2,1,0:T(8,128)S(1)}, f32[2,64,256]{2,0,1:T(2,128)S(1)}, /*index=5*/s32[]{:T(128)}, s32[]{:T(128)}) while((s32[]{:T(128)}, f32[2,64,256]{2,0,1:T(2,128)S(1)}, f32[2,64,64]{2,1,0:T(8,128)S(1)}, f32[2,64,256]{2,1,0:T(8,128)S(1)}, ...), condition=%wide.region_4.4_spmd, body=%wide.region_2.3_spmd.sunk | while | flops 7323650 | bytes 901221 | solution.py:54
  93.8 1.5 fusion.80
  100.8 7.7 %psum.53 = f32[128]{0:T(128)S(1)} all-reduce(f32[128]{0:T(128)S(1)} %reshape.121), channel_id=1, replica_groups=mesh['tiles'=2,'rows'=4,'rep'=2,'sub'=2] {'rep','sub'}, use_global_device_ids=true, to_apply=%region_8.9 | all-reduce | flops 128 | bytes 1024 | tf_op jit(solution)/shard_map/psum | solution.py:113
  108.8 20.0 %while.88 = (s32[]{:T(128)}, f32[2,64,256]{2,0,1:T(2,128)S(1)}, f32[2,128,256]{2,1,0:T(8,128)S(1)}, bf16[2,2,2]{2,1,0:T(2,128)(2,1)S(1)}, f32[2,2,64,256]{3,2,1,...) while((s32[]{:T(128)}, f32[2,64,256]{2,0,1:T(2,128)S(1)}, ...), condition=%wide.region_14.15_spmd.clone.clone, body=%wide.region_9.14_spmd.clone.sunk.clone | while | flops 14319621 | bytes 3786608 | solution.py:131
  109.2 8.6 %while.87 = (s32[]{:T(128)}, f32[2,64,256]{2,0,1:T(2,128)S(1)}, f32[2,64,256]{2,0,1:T(2,128)S(1)}, f32[2,64,64]{2,1,0:T(8,128)S(1)}, f32[2,64,256]{2,1,0:T(8,128...) while((s32[]{:T(128)}, f32[2,64,256]{2,0,1:T(2,128)S(1)}, ...), condition=%wide.region_13.13_spmd, body=%wide.region_10.12_spmd.sunk | while | flops 12550146 | bytes 1425529 | solution.py:54
  109.3 2.2 fusion.79
  113.6 2.2 fusion.79
  119.1 8.6 %while.87 = (s32[]{:T(128)}, f32[2,64,256]{2,0,1:T(2,128)S(1)}, f32[2,64,256]{2,0,1:T(2,128)S(1)}, f32[2,64,64]{2,1,0:T(8,128)S(1)}, f32[2,64,256]{2,1,0:T(8,128...) while((s32[]{:T(128)}, f32[2,64,256]{2,0,1:T(2,128)S(1)}, ...), condition=%wide.region_13.13_spmd, body=%wide.region_10.12_spmd.sunk | while | flops 12550146 | bytes 1425529 | solution.py:54
  119.3 2.2 fusion.79
  123.6 2.2 fusion.79
  129.5 14.2 %while.84 = (s32[]{:T(128)}, f32[128,256]{1,0:T(8,128)S(1)}, s32[]{:T(128)}, s32[]{:T(128)}, f32[2,128,256]{2,1,0:T(8,128)S(1)}) while((s32[]{:T(128)}, f32[128,256]{1,0:T(8,128)S(1)}, s32[]{:T(128)}, s32[]{:T(128)}, f32[2,128,256]{2,1,0:T(8,128)S(1)}) %tuple.175), condition=%wide.region_17.18_spmd.clone, body=%wide.region_16.17_spmd.sunk.clone | while | flops 65573 | bytes 917961 | solution.py:154
  130.5 2.8 %collective-permute-done = f32[128,256]{1,0:T(8,128)S(1)} collective-permute-done((f32[128,256]{1,0:T(8,128)S(1)}, f32[128,256]{1,0:T(8,128)S(1)}, u32[]{:S(2)}, u32[]{:S(2)}) %collective-permute-start) | collective-permute-done | bytes 131104 | tf_op jit(solution)/shard_map/while/body/eval_jaxpr/ppermute | solution.py:14
  134.4 3.5 %collective-permute-done = f32[128,256]{1,0:T(8,128)S(1)} collective-permute-done((f32[128,256]{1,0:T(8,128)S(1)}, f32[128,256]{1,0:T(8,128)S(1)}, u32[]{:S(2)}, u32[]{:S(2)}) %collective-permute-start) | collective-permute-done | bytes 131104 | tf_op jit(solution)/shard_map/while/body/eval_jaxpr/ppermute | solution.py:14
  138.3 5.3 %collective-permute-done = f32[128,256]{1,0:T(8,128)S(1)} collective-permute-done((f32[128,256]{1,0:T(8,128)S(1)}, f32[128,256]{1,0:T(8,128)S(1)}, u32[]{:S(2)}, u32[]{:S(2)}) %collective-permute-start) | collective-permute-done | bytes 131104 | tf_op jit(solution)/shard_map/while/body/eval_jaxpr/ppermute | solution.py:14
  144.4 36.1 %all-reduce.6.cloned.1.call-done = (f32[128,256]{1,0:T(8,128)}, f32[128,256]{1,0:T(8,128)}, f32[128,256]{1,0:T(8,128)}) async-done(((f32[128,256]{1,0:T(8,128)}, f32[128,256]{1,0:T(8,128)}, f32[128,256]{1,0:T(8,128)}), (f32[128,256]{1,0:T(8,128)}, f32[128,256]{1,0:T(8,128)}, f32[128,256]{1,0:T(8,128)})) %all-reduce.6.cloned.1.call-update) | async-done | bytes 393232 | tf_op jit(solution)/shard_map/psum | solution.py:113
  180.5 1.8 add_convert_fusion
  185.2 37.4 %all-reduce.8.cloned.1.call-done = (f32[256,256]{0,1:T(8,128)}, f32[256,256]{0,1:T(8,128)}) async-done(((f32[256,256]{0,1:T(8,128)}, f32[256,256]{0,1:T(8,128)}), (f32[256,256]{0,1:T(8,128)}, f32[256,256]{0,1:T(8,128)})) %all-reduce.8.cloned.1.call-update) | async-done | bytes 524304 | tf_op jit(solution)/shard_map/psum | solution.py:170
  222.6 1.8 copy.82
  (158 shorter events, 34.8 us)
Async XLA Ops:
  8.0 1.5 copy-start
  8.0 1.1 copy-start.5
  8.0 1.2 copy-start.8
  8.0 1.4 copy-start.7
  9.9 0.7 copy-start.9
  9.9 0.9 copy-start.3
  11.0 36.9 %all-reduce.10.cloned.1.call-start = ((), (), s32[]{:S(2)}) async-start(), calls=%async_computation.2 | async-start | bytes 131072 | tf_op jit(solution)/shard_map/while/body/eval_jaxpr/psum | solution.py:9
  54.2 0.8 copy-start.1
  55.0 37.6 %all-reduce.10.cloned.1.call-start = ((), (), s32[]{:S(2)}) async-start(), calls=%async_computation.2 | async-start | bytes 131072 | tf_op jit(solution)/shard_map/while/body/eval_jaxpr/psum | solution.py:9
  98.8 0.8 copy-start.1
  99.7 8.7 %copy-start.2 = (f32[128,256]{1,0:T(8,128)S(1)}, f32[128,256]{1,0:T(8,128)}, u32[]{:S(2)}) copy-start(f32[128,256]{1,0:T(8,128)} %param.20) | copy-start | bytes 393220
  99.7 80.8 %all-reduce.6.cloned.1.call-start = ((), (), s32[]{:S(2)}) async-start(), calls=%async_computation | async-start | bytes 786432 | tf_op jit(solution)/shard_map/psum | solution.py:113
  129.5 3.9 %collective-permute-start = (f32[128,256]{1,0:T(8,128)S(1)}, f32[128,256]{1,0:T(8,128)S(1)}, u32[]{:S(2)}, u32[]{:S(2)}) collective-permute-start(f32[128,256]{1,0:T(8,128)S(1)} %get-tuple-element.1202), channel_id=1, source_target_pairs={{0,4},{4,8},{8,12},{12,0},{1,5},{5,9},{9,13},{13,1},{2,6},{6,10},{... | collective-permute-start | bytes 393224 | tf_op jit(solution)/shard_map/while/body/eval_jaxpr/ppermute | solution.py:14
  133.4 4.5 %collective-permute-start = (f32[128,256]{1,0:T(8,128)S(1)}, f32[128,256]{1,0:T(8,128)S(1)}, u32[]{:S(2)}, u32[]{:S(2)}) collective-permute-start(f32[128,256]{1,0:T(8,128)S(1)} %get-tuple-element.1202), channel_id=1, source_target_pairs={{0,4},{4,8},{8,12},{12,0},{1,5},{5,9},{9,13},{13,1},{2,6},{6,10},{... | collective-permute-start | bytes 393224 | tf_op jit(solution)/shard_map/while/body/eval_jaxpr/ppermute | solution.py:14
  138.0 5.7 %collective-permute-start = (f32[128,256]{1,0:T(8,128)S(1)}, f32[128,256]{1,0:T(8,128)S(1)}, u32[]{:S(2)}, u32[]{:S(2)}) collective-permute-start(f32[128,256]{1,0:T(8,128)S(1)} %get-tuple-element.1202), channel_id=1, source_target_pairs={{0,4},{4,8},{8,12},{12,0},{1,5},{5,9},{9,13},{13,1},{2,6},{6,10},{... | collective-permute-start | bytes 393224 | tf_op jit(solution)/shard_map/while/body/eval_jaxpr/ppermute | solution.py:14
  143.7 0.7 copy-start.4
  144.4 78.2 %all-reduce.8.cloned.1.call-start = ((), (), s32[]{:S(2)}) async-start(), calls=%async_computation.1 | async-start | bytes 1048576 | tf_op jit(solution)/shard_map/psum | solution.py:170
  222.6 1.8 copy-start.6
Sparse Core Ops, SparseCore 0:
  14.9 33.0 all-reduce.9
  58.9 33.6 all-reduce.9
Sparse Core Ops, SparseCore 1:
  144.4 36.0 all-reduce.5
  184.2 38.3 all-reduce.7
where the time goes:
time: 237 us; the launch traced here: 233 us
  waiting for transfers between devices  156 us (66%)
  local copies, waits for them, and re-layouts  20.1 us (8%)
  other arithmetic  19 us (8%)
  between operations  15.7 us (7%)
  matrix products  9.6 us (4%)
  blocking collectives  7.66 us (3%)
  starting transfers between devices  2.63 us (1%)
    psum x2, waiting for transfers between devices, spread(): return lax.psum(kept, axis)  70.4 us
    psum x1, waiting for transfers between devices, body(): lax.psum((center_local, neighbor_local), 'rows')  37.4 us
    psum x1, waiting for transfers between devices, body(): lax.psum((running.reshape(points, feat_width), counts), ('rep', 'sub'))  36.1 us
    dynamic_update_slice x24, local copies, waits for them, and re-layouts, tile_loop(): return lax.map(visit, (tile_flags, members))  11.8 us
    ppermute x3, waiting for transfers between devices, passed_along(): lax.ppermute(x, axis, [(i, (i + by) % length) for i in range(length)])  11.6 us
    reduce_sum x4, other arithmetic, edge_gradients(): return (jnp.sum(slopes, axis=1), jnp.sum(slopes, axis=0))  8.64 us
    psum x1, blocking collectives, body(): lax.psum((running.reshape(points, feat_width), counts), ('rep', 'sub'))  7.66 us
    reduce_sum x4, other arithmetic, edge_total(): return (jnp.sum(link_tile[:, :, None] * jax.nn.silu(pre_act), axis=1),)  5.84 us
  transfers between devices with their start and end apart: 7, of which 7 were waited for; matrix products, arithmetic and copies ran while one was open for 0% of the time, Pallas kernels for 0%

commit v1 on v0

v1 whole, which is shorter than its diff:
```python
import functools

import jax
import jax.numpy as jnp
from jax import lax
from jax.experimental import pallas as pl
from jax.experimental.pallas import tpu as pltpu
from jax.sharding import PartitionSpec as P

F32 = jnp.float32
BF16 = jnp.bfloat16
MESH = pl.DeviceIdType.MESH
LANES = 4


def dot(a, b, dims=((1,), (0,))):
    return lax.dot_general(a, b, (dims, ((), ())), preferred_element_type=F32)


def kernel(
    sizes,
    rows_s,
    cols_s,
    feat_ref,
    wc_ref,
    wn_ref,
    cot_ref,
    links_ref,
    eo_ref,
    fg_ref,
    cg_ref,
    ng_ref,
    fh_all,
    halves,
    center,
    nown,
    scale,
    degree,
    npanel,
    a4_ref,
    near_s,
    near_d,
    far_acc,
    c_tile,
    s_tile,
    e_acc,
    f_acc,
    near_out,
    far_out,
    near_in,
    far_in,
    cnt,
    eo_all,
    fh_send,
    fh_recv,
    cnt_send,
    cnt_recv,
    near_send,
    near_recv,
    far_send,
    far_recv,
    row_send,
    row_recv,
    grp_send,
    grp_recv,
    eo_send,
    eo_recv,
):
    R, C, S, U, Q, B = sizes
    G = C * S
    points, feat = feat_ref.shape
    nblk = points // B
    sl = points // G
    step = B // LANES
    t_id = lax.axis_index("tiles")
    r = lax.axis_index("rows")
    c = lax.axis_index("rep")
    s = lax.axis_index("sub")
    p = c * S + s

    def dev(row, member):
        return (t_id, row, member // S, member % S)

    barrier = pltpu.get_barrier_semaphore()

    def greet(n, carry):
        other = (r * G + p + n) % (R * G)
        pl.semaphore_signal(
            barrier, inc=1, device_id=dev(other // G, other % G), device_id_type=MESH
        )
        return carry

    lax.fori_loop(1, R * G, greet, 0)

    def own_rows(owner):
        return pl.ds(pl.multiple_of(owner * points, points), points)

    def slice_rows(member):
        return pl.ds(pl.multiple_of(member * sl, sl), sl)

    def hall_rows(owner, member):
        return pl.ds(pl.multiple_of(owner * points + member * sl, sl), sl)

    fh = feat_ref[...].astype(BF16)
    fh_all[own_rows(r), :] = fh

    count = [jnp.zeros((8, B), F32) for _ in range(nblk)]
    for t in range(U * Q):
        tile = links_ref[t].astype(F32)
        a4_ref[t] = jnp.concatenate([tile[m * step : (m + 1) * step] for m in range(LANES)], axis=1)
        row_sum = dot(jnp.ones((8, B), BF16), tile.astype(BF16), ((1,), (1,)))
        block = rows_s[t] - r * nblk
        count = [count[n] + jnp.where(jnp.full(row_sum.shape, block, jnp.int32) == n, row_sum, 0.0) for n in range(nblk)]
    cnt[pl.ds(p, 1)] = jnp.concatenate(count, axis=1)[None]

    pl.semaphore_wait(barrier, R * G - 1)

    def fh_copy(n):
        to = (r + n) % R
        return pltpu.make_async_remote_copy(
            src_ref=fh_all.at[own_rows(r)],
            dst_ref=fh_all.at[own_rows(r)],
            send_sem=fh_send.at[n],
            recv_sem=fh_recv.at[r],
            device_id=dev(to, p),
            device_id_type=MESH,
        )

    def fh_wait(owner):
        pltpu.make_async_remote_copy(
            src_ref=fh_all.at[own_rows(owner)],
            dst_ref=fh_all.at[own_rows(owner)],
            send_sem=fh_send.at[0],
            recv_sem=fh_recv.at[owner],
            device_id=dev(r, p),
            device_id_type=MESH,
        ).wait_recv()

    def member_copy(src, dst, send_sem, recv_sem, n, owner=None):
        return pltpu.make_async_remote_copy(
            src_ref=src,
            dst_ref=dst,
            send_sem=send_sem,
            recv_sem=recv_sem,
            device_id=dev(r if owner is None else owner, (p + n) % G),
            device_id_type=MESH,
        )

    cnt_copies = [
        member_copy(cnt.at[p], cnt.at[p], cnt_send.at[n], cnt_recv.at[p], n) for n in range(1, G)
    ]
    for copy in cnt_copies:
        copy.start()

    @pl.when(r % C == c)
    def _():
        for n in range(1, R):
            fh_copy(n).start()

    cc = dot(fh, wc_ref[...]).astype(BF16).astype(F32) * 0.5
    center[...] = cc
    nn = dot(fh, wn_ref[...]).astype(BF16).astype(F32) * 0.5
    nown[...] = nn

    for n in range(1, G):
        member = (p + n) % G
        member_copy(cnt.at[member], cnt.at[member], cnt_send.at[0], cnt_recv.at[member], 1).wait_recv()
    total = cnt[0]
    for m in range(1, G):
        total = total + cnt[m]
    wide = jnp.concatenate(
        [jnp.transpose(jnp.broadcast_to(total[0:1, h : h + 128], (128, 128))) for h in range(0, points, 128)],
        axis=0,
    )
    deg = jnp.concatenate([wide] * (feat // 128), axis=1) + 1.0
    degree[...] = deg
    scale[...] = (cot_ref[...] / deg).astype(BF16).astype(F32)

    @pl.when(r % C != c)
    def _():
        for n in range(1, R):
            fh_copy(n).start()

    e_acc[...] = jnp.zeros_like(e_acc)
    f_acc[...] = jnp.zeros_like(f_acc)

    lane_m = lax.broadcasted_iota(jnp.int32, (16, LANES * B), 1) // B
    near_mask = jnp.where(
        lax.broadcasted_iota(jnp.int32, (16, LANES * B), 0) == lane_m, 1.0, 0.0
    ).astype(BF16)
    eye_mask = jnp.where(
        lax.broadcasted_iota(jnp.int32, (B, LANES * B), 1) % B
        == lax.broadcasted_iota(jnp.int32, (B, LANES * B), 0),
        1.0,
        0.0,
    ).astype(BF16)

    def in_order(ref):
        return jnp.concatenate(
            [
                jnp.concatenate([ref[k, pl.ds(m, step, stride=8), :] for m in range(LANES)], axis=0)
                for k in range(feat // 128)
            ],
            axis=1,
        )

    def chosen(block, n, value):
        return jnp.where(jnp.full(value.shape, block, jnp.int32) == n, value, 0.0)

    def picked(ref, block):
        value = chosen(block, 0, ref[0:B, :])
        for n in range(1, nblk):
            value = value + chosen(block, n, ref[n * B : (n + 1) * B, :])
        return value

    def section(u):
        owner = u * C + c

        @pl.when(owner != r)
        def _():
            fh_wait(owner)

        npanel[...] = dot(fh_all[own_rows(owner), :], wn_ref[...]).astype(BF16).astype(F32) * 0.5

        for q in range(Q):
            t = u * Q + q
            row_block = rows_s[t] - r * nblk
            col_block = cols_s[t] % nblk
            nval = picked(npanel, col_block).astype(BF16).reshape(B // 16, 16, feat)
            far_acc[...] = jnp.zeros_like(far_acc)
            c_tile[...] = picked(center, row_block)
            s_tile[...] = picked(scale, row_block) * 0.5

            def group(g, carry):
                sil, slo = [], []
                for m in range(LANES):
                    at = pl.ds(g + m * step, 1)
                    crow = jnp.broadcast_to(c_tile[at, :], (16, feat)).astype(BF16)
                    srow = jnp.broadcast_to(s_tile[at, :], (16, feat)).astype(BF16)
                    h = nval + crow[None]
                    th = jnp.tanh(h)
                    one = 1.0 + th
                    sil.append((h * one).reshape(B, feat))
                    slo.append((one * (1.0 + (h - h * th)) * srow[None]).reshape(B, feat))
                sil = jnp.concatenate(sil, axis=0)
                slo = jnp.concatenate(slo, axis=0)
                arow = jnp.broadcast_to(a4_ref[t, pl.ds(g, 1), :], (16, LANES * B)).astype(BF16)
                near_l = near_mask * arow
                far_l = (eye_mask.reshape(B // 16, 16, LANES * B) * arow[None]).reshape(B, LANES * B)
                out_s = dot(near_l, sil)
                out_d = dot(jnp.concatenate([near_l, far_l], axis=0), slo)
                at8 = pl.ds(pl.multiple_of(g * 8, 8), 8)
                for k in range(feat // 128):
                    near_s[k, at8, :] = out_s[0:8, k * 128 : (k + 1) * 128]
                    near_d[k, at8, :] = out_d[0:8, k * 128 : (k + 1) * 128]
                far_acc[...] += out_d[16:]
                return carry

            lax.fori_loop(0, step, group, 0)
            tile_e, tile_c = in_order(near_s), in_order(near_d)
            far = far_acc[...]
            for n in range(nblk):
                block = slice(n * B, (n + 1) * B)
                e_acc[0, block, :] += chosen(row_block, n, tile_e)
                e_acc[1, block, :] += chosen(row_block, n, tile_c)
                if q == 0:
                    f_acc[block, :] = chosen(col_block, n, far)
                else:
                    f_acc[block, :] += chosen(col_block, n, far)

        far_out[u] = f_acc[...].astype(BF16)

        def far_copy(n):
            member = (p + n) % G
            return member_copy(
                far_out.at[u, slice_rows(member)],
                far_in.at[r * S + s],
                far_send.at[u * G + n],
                far_recv.at[r * S + s],
                n,
                owner,
            )

        for n in range(1, G):
            far_copy(n).start()

        @pl.when(owner != r)
        def _():
            far_copy(0).start()

        @pl.when(owner == r)
        def _():
            far_in[pl.ds(r * S + s, 1)] = far_out[u, slice_rows(p), :][None]

        return far_copy

    far_copies = [section(u) for u in range(U)]

    near_out[...] = e_acc[...].astype(BF16)
    near_copies = [
        member_copy(
            near_out.at[:, slice_rows((p + n) % G)],
            near_in.at[p],
            near_send.at[n],
            near_recv.at[p],
            n,
        )
        for n in range(1, G)
    ]
    for copy in near_copies:
        copy.start()

    mine = slice_rows(p)
    cs, ns = center[mine, :], nown[mine, :]
    sc, dg = scale[mine, :], degree[mine, :]
    self_h = cs + ns
    self_t = jnp.tanh(self_h)
    self_silu = self_h * (1.0 + self_t)
    self_slope = sc * 0.5 * (1.0 + self_t) * (1.0 + self_h * (1.0 - self_t))
    e_sum = e_acc[0, mine, :] + self_silu
    c_sum = e_acc[1, mine, :] + self_slope
    for n in range(1, G):
        member = (p + n) % G
        member_copy(
            near_out.at[:, mine], near_in.at[member], near_send.at[0], near_recv.at[member], 1
        ).wait_recv()
        arrived = near_in[pl.ds(member, 1)][0]
        e_sum = e_sum + arrived[0].astype(F32)
        c_sum = c_sum + arrived[1].astype(F32)
    eo_all[mine, :] = (e_sum / dg).astype(BF16)
    eo_copies = [
        member_copy(eo_all.at[mine], eo_all.at[mine], eo_send.at[n], eo_recv.at[p], n)
        for n in range(1, G)
    ]
    for copy in eo_copies:
        copy.start()

    n_sum = self_slope
    for row in range(R):
        for sub in range(S):
            slot = row * S + sub
            here = (row == r) & (sub == s) & (r % C == c)

            @pl.when(jnp.logical_not(here))
            def _():
                member_copy(
                    far_out.at[0, mine], far_in.at[slot], far_send.at[0], far_recv.at[slot], 1
                ).wait_recv()

            n_sum = n_sum + far_in[slot].astype(F32)

    def own_part(owner, member):
        return halves.at[:, hall_rows(owner, member)]

    halves[0, hall_rows(r, p), :] = c_sum.astype(BF16)
    halves[1, hall_rows(r, p), :] = n_sum.astype(BF16)

    def row_copy(n):
        return pltpu.make_async_remote_copy(
            src_ref=own_part(r, p),
            dst_ref=own_part(r, p),
            send_sem=row_send.at[n],
            recv_sem=row_recv.at[r],
            device_id=dev((r + n) % R, p),
            device_id_type=MESH,
        )

    def relay_copy(n_row, n):
        owner = (r + n_row) % R
        return member_copy(
            own_part(owner, p),
            own_part(owner, p),
            grp_send.at[n_row * G + n],
            grp_recv.at[owner * G + p],
            n,
        )

    for n in range(1, R):
        row_copy(n).start()
    for n in range(1, G):
        relay_copy(0, n).start()
    for n_row in range(1, R):
        owner = (r + n_row) % R
        pltpu.make_async_remote_copy(
            src_ref=own_part(owner, p),
            dst_ref=own_part(owner, p),
            send_sem=row_send.at[0],
            recv_sem=row_recv.at[owner],
            device_id=dev(r, p),
            device_id_type=MESH,
        ).wait_recv()
        for n in range(1, G):
            relay_copy(n_row, n).start()

    for n in range(1, G):
        member = (p + n) % G
        rows = slice_rows(member)
        member_copy(eo_all.at[rows], eo_all.at[rows], eo_send.at[0], eo_recv.at[member], 1).wait_recv()
    eo_ref[...] = eo_all[...].astype(F32)

    def grp_wait(owner):
        for n in range(1, G):
            member = (p + n) % G
            member_copy(
                own_part(owner, member),
                own_part(owner, member),
                grp_send.at[0],
                grp_recv.at[owner * G + member],
                1,
            ).wait_recv()

    grp_wait(r)
    fg_ref[...] = dot(halves[0, own_rows(r), :], wc_ref[...], ((1,), (1,))) + dot(
        halves[1, own_rows(r), :], wn_ref[...], ((1,), (1,))
    )
    for n in range(1, R):
        owner = (r + n) % R

        @pl.when(owner % C != c)
        def _():
            fh_wait(owner)

    for n in range(1, R):
        grp_wait((r + n) % R)
    cg_ref[...] = dot(fh_all[...], halves[0], ((0,), (0,)))
    ng_ref[...] = dot(fh_all[...], halves[1], ((0,), (0,)))

    for n in range(1, R):
        fh_copy(n).wait_send()
        row_copy(n).wait_send()
    for copy in cnt_copies + near_copies + eo_copies:
        copy.wait_send()
    for n_row in range(R):
        for n in range(1, G):
            relay_copy(n_row, n).wait_send()
    for u in range(U):
        for n in range(1, G):
            far_copies[u](n).wait_send()

        @pl.when(u * C + c != r)
        def _():
            far_copies[u](0).wait_send()


def body(features, center_weight, neighbor_weight, cotangent, tile_rows, tile_cols, tile_links):
    R, C, S = lax.axis_size("rows"), lax.axis_size("rep"), lax.axis_size("sub")
    U = R // C
    T, B = tile_rows.shape[0], tile_links.shape[1]
    points, feat = features.shape
    G = C * S
    sl = points // G
    sizes = (R, C, S, U, T // U, B)
    step = B // LANES
    dma = pltpu.SemaphoreType.DMA
    vm = pltpu.VMEM
    out = jax.ShapeDtypeStruct
    return pl.pallas_call(
        functools.partial(kernel, sizes),
        out_shape=(
            out((points, feat), F32),
            out((points, feat), F32),
            out((feat, feat), F32),
            out((feat, feat), F32),
        ),
        in_specs=[pl.BlockSpec(memory_space=pltpu.SMEM)] * 2
        + [pl.BlockSpec(memory_space=pltpu.VMEM)] * 5,
        out_specs=[pl.BlockSpec(memory_space=pltpu.VMEM)] * 4,
        scratch_shapes=[
            vm((R * points, feat), BF16),
            vm((2, R * points, feat), BF16),
            vm((points, feat), F32),
            vm((points, feat), F32),
            vm((points, feat), F32),
            vm((points, feat), F32),
            vm((points, feat), F32),
            vm((T, step, LANES * B), F32),
            vm((feat // 128, step * 8, 128), F32),
            vm((feat // 128, step * 8, 128), F32),
            vm((B, feat), F32),
            vm((B, feat), F32),
            vm((B, feat), F32),
            vm((2, points, feat), F32),
            vm((points, feat), F32),
            vm((2, points, feat), BF16),
            vm((U, points, feat), BF16),
            vm((G, 2, sl, feat), BF16),
            vm((R * S, sl, feat), BF16),
            vm((G, 8, points), F32),
            vm((points, feat), BF16),
            dma((R,)),
            dma((R,)),
            dma((G,)),
            dma((G,)),
            dma((G,)),
            dma((G,)),
            dma((U * G,)),
            dma((R * S,)),
            dma((R,)),
            dma((R,)),
            dma((R * G,)),
            dma((R * G,)),
            dma((G,)),
            dma((G,)),
        ],
        compiler_params=pltpu.CompilerParams(
            collective_id=0, has_side_effects=True, vmem_limit_bytes=48 * 1024 * 1024
        ),
    )(tile_rows, tile_cols, features, center_weight, neighbor_weight, cotangent, tile_links)


def solution(mesh):
    in_specs = (
        P(("tiles", "rows"), None),
        P(),
        P(),
        P(("tiles", "rows"), None),
        P(("tiles", "rows", "rep", "sub")),
        P(("tiles", "rows", "rep", "sub")),
        P(("tiles", "rows", "rep", "sub"), None, None),
    )
    out_specs = (
        P(("tiles", "rows"), None),
        P(("tiles", "rows"), None),
        P("tiles", None),
        P("tiles", None),
    )
    return jax.shard_map(body, mesh=mesh, in_specs=in_specs, out_specs=out_specs, check_vma=False)
```

time: 237 us -> 49.3 us (0.21)
  the two profiles are of different devices: /device:TPU:11 before, /device:TPU:0 now
where the time goes in v1:
time: 49.3 us; the launch traced here: 49.1 us
  Pallas kernels  39.9 us (81%)
  local copies, waits for them, and re-layouts  8.54 us (17%)
  between operations  0.66 us (1%)
    pallas_call x1, Pallas kernels, body(): pl.pallas_call(functools.partial(kernel, sizes), out_shape=(out((points,...  39.9 us
    unnamed x18, local copies, waits for them, and re-layouts  8.54 us

profile of v1, /device:TPU:0, one launch (start us, length us, event | category | flops | bytes accessed | tf_op | source)
XLA Modules:
  0.0 49.1 jit_solution(14919031655536360384)
XLA Ops:
  0.6 0.0 copy-start
  0.6 0.9 %copy-done = f32[128,256]{1,0:T(8,128)S(1)} copy-done((f32[128,256]{1,0:T(8,128)S(1)}, f32[128,256]{1,0:T(8,128)}, u32[]{:S(2)}) %copy-start) | copy-done | bytes 131096
  1.5 0.0 copy-start.1
  1.5 0.9 %copy-done.1 = bf16[256,256]{1,0:T(8,128)(2,1)S(1)} copy-done((bf16[256,256]{1,0:T(8,128)(2,1)S(1)}, bf16[256,256]{1,0:T(8,128)(2,1)}, u32[]{:S(2)}) %copy-start.1) | copy-done | bytes 131096
  2.4 0.0 copy-start.2
  2.4 0.9 %copy-done.2 = bf16[256,256]{1,0:T(8,128)(2,1)S(1)} copy-done((bf16[256,256]{1,0:T(8,128)(2,1)S(1)}, bf16[256,256]{1,0:T(8,128)(2,1)}, u32[]{:S(2)}) %copy-start.2) | copy-done | bytes 131096
  3.3 0.0 copy-start.3
  3.4 0.9 %copy-done.3 = f32[128,256]{1,0:T(8,128)S(1)} copy-done((f32[128,256]{1,0:T(8,128)S(1)}, f32[128,256]{1,0:T(8,128)}, u32[]{:S(2)}) %copy-start.3) | copy-done | bytes 131096
  4.3 0.0 copy-start.4
  4.3 0.9 %copy-done.4 = s32[4,64,64]{2,1,0:T(8,128)S(1)} copy-done((s32[4,64,64]{2,1,0:T(8,128)S(1)}, s32[4,64,64]{2,1,0:T(8,128)}, u32[]{:S(2)}) %copy-start.4) | copy-done | bytes 65560
  5.2 0.0 copy-start.5
  5.2 0.7 %copy-done.5 = s32[4]{0:T(128)S(1)} copy-done((s32[4]{0:T(128)S(1)}, s32[4]{0:T(128)}, u32[]{:S(2)}) %copy-start.5) | copy-done | bytes 40
  5.8 0.0 copy-start.6
  5.8 0.7 %copy-done.6 = s32[4]{0:T(128)S(1)} copy-done((s32[4]{0:T(128)S(1)}, s32[4]{0:T(128)}, u32[]{:S(2)}) %copy-start.6) | copy-done | bytes 40
  6.5 39.9 %shard_map.102 = (f32[128,256]{1,0:T(8,128)S(1)}, f32[128,256]{1,0:T(8,128)S(1)}, f32[256,256]{1,0:T(8,128)S(1)}, f32[256,256]{1,0:T(8,128)S(1)}) custom-call(s32[4]{0:T(128)S(1)} %copy-done.5, s32[4]{0:T(128)S(1)} %copy-done.6, f32[128,256]{1,0:T(8,128)S(1)} %copy-done, bf16[256,256]{1,0:T(8,128)(2,1)S(1)} %copy-done.1, bf16[256,256]{1,0:T(8,128)(2,1)S(1)} %copy-done.2, ...), custom_call_target="tpu_custom_call" | custom-call | tf_op jit(solution)/shard_map/pallas_call | solution.py:457
  46.3 0.7 %copy.15 = f32[128,256]{1,0:T(8,128)} copy(f32[128,256]{1,0:T(8,128)S(1)} %get-tuple-element.8) | data formatting | bytes 262144
  47.0 0.7 %copy.16 = f32[128,256]{1,0:T(8,128)} copy(f32[128,256]{1,0:T(8,128)S(1)} %get-tuple-element.9) | data formatting | bytes 262144
  47.7 0.7 %copy.17 = f32[256,256]{1,0:T(8,128)} copy(f32[256,256]{1,0:T(8,128)S(1)} %get-tuple-element.10) | data formatting | bytes 524288
  48.4 0.7 %copy.18 = f32[256,256]{1,0:T(8,128)} copy(f32[256,256]{1,0:T(8,128)S(1)} %get-tuple-element.11) | data formatting | bytes 524288
Async XLA Ops:
  0.6 0.9 %copy-start = (f32[128,256]{1,0:T(8,128)S(1)}, f32[128,256]{1,0:T(8,128)}, u32[]{:S(2)}) copy-start(f32[128,256]{1,0:T(8,128)} %feat_ref.1) | copy-start | bytes 393220
  1.5 0.9 %copy-start.1 = (bf16[256,256]{1,0:T(8,128)(2,1)S(1)}, bf16[256,256]{1,0:T(8,128)(2,1)}, u32[]{:S(2)}) copy-start(bf16[256,256]{1,0:T(8,128)(2,1)} %wc_ref.1) | copy-start | bytes 393220
  2.4 0.9 %copy-start.2 = (bf16[256,256]{1,0:T(8,128)(2,1)S(1)}, bf16[256,256]{1,0:T(8,128)(2,1)}, u32[]{:S(2)}) copy-start(bf16[256,256]{1,0:T(8,128)(2,1)} %wn_ref.1) | copy-start | bytes 393220
  3.3 0.9 %copy-start.3 = (f32[128,256]{1,0:T(8,128)S(1)}, f32[128,256]{1,0:T(8,128)}, u32[]{:S(2)}) copy-start(f32[128,256]{1,0:T(8,128)} %cot_ref.1) | copy-start | bytes 393220
  4.3 0.9 %copy-start.4 = (s32[4,64,64]{2,1,0:T(8,128)S(1)}, s32[4,64,64]{2,1,0:T(8,128)}, u32[]{:S(2)}) copy-start(s32[4,64,64]{2,1,0:T(8,128)} %links_ref.1) | copy-start | bytes 196612
  5.2 0.7 %copy-start.5 = (s32[4]{0:T(128)S(1)}, s32[4]{0:T(128)}, u32[]{:S(2)}) copy-start(s32[4]{0:T(128)} %rows_s.1) | copy-start | bytes 52
  5.8 0.7 %copy-start.6 = (s32[4]{0:T(128)S(1)}, s32[4]{0:T(128)}, u32[]{:S(2)}) copy-start(s32[4]{0:T(128)} %cols_s.1) | copy-start | bytes 52

commit v2 on v1

--- a/solution.py
+++ b/solution.py
@@ -19,6 +19,17 @@
 
 def kernel(
     sizes,
+    rows_h,
+    cols_h,
+    feat_h,
+    wc_h,
+    wn_h,
+    cot_h,
+    links_h,
+    eo_ref,
+    fg_ref,
+    cg_ref,
+    ng_ref,
     rows_s,
     cols_s,
     feat_ref,
@@ -26,10 +37,7 @@
     wn_ref,
     cot_ref,
     links_ref,
-    eo_ref,
-    fg_ref,
-    cg_ref,
-    ng_ref,
+    in_sem,
     fh_all,
     halves,
     center,
@@ -81,6 +89,23 @@
     def dev(row, member):
         return (t_id, row, member // S, member % S)
 
+    loads = [
+        pltpu.make_async_copy(src, dst, in_sem.at[k])
+        for k, (src, dst) in enumerate(
+            (
+                (feat_h, feat_ref),
+                (links_h, links_ref),
+                (rows_h, rows_s),
+                (cols_h, cols_s),
+                (wc_h, wc_ref),
+                (wn_h, wn_ref),
+                (cot_h, cot_ref),
+            )
+        )
+    ]
+    for load in loads:
+        load.start()
+
     barrier = pltpu.get_barrier_semaphore()
 
     def greet(n, carry):
@@ -101,8 +126,12 @@
     def hall_rows(owner, member):
         return pl.ds(pl.multiple_of(owner * points + member * sl, sl), sl)
 
+    loads[0].wait()
     fh = feat_ref[...].astype(BF16)
     fh_all[own_rows(r), :] = fh
+
+    for load in loads[1:4]:
+        load.wait()
 
     count = [jnp.zeros((8, B), F32) for _ in range(nblk)]
     for t in range(U * Q):
@@ -157,6 +186,8 @@
         for n in range(1, R):
             fh_copy(n).start()
 
+    for load in loads[4:]:
+        load.wait()
     cc = dot(fh, wc_ref[...]).astype(BF16).astype(F32) * 0.5
     center[...] = cc
     nn = dot(fh, wn_ref[...]).astype(BF16).astype(F32) * 0.5
@@ -241,7 +272,7 @@
                     th = jnp.tanh(h)
                     one = 1.0 + th
                     sil.append((h * one).reshape(B, feat))
-                    slo.append((one * (1.0 + (h - h * th)) * srow[None]).reshape(B, feat))
+                    slo.append((one * (1.0 + h * (1.0 - th)) * srow[None]).reshape(B, feat))
                 sil = jnp.concatenate(sil, axis=0)
                 slo = jnp.concatenate(slo, axis=0)
                 arow = jnp.broadcast_to(a4_ref[t, pl.ds(g, 1), :], (16, LANES * B)).astype(BF16)
@@ -256,7 +287,7 @@
                 far_acc[...] += out_d[16:]
                 return carry
 
-            lax.fori_loop(0, step, group, 0)
+            lax.fori_loop(0, step, group, 0, unroll=4)
             tile_e, tile_c = in_order(near_s), in_order(near_d)
             far = far_acc[...]
             for n in range(nblk):
@@ -365,32 +396,58 @@
             device_id_type=MESH,
         )
 
-    def relay_copy(n_row, n):
-        owner = (r + n_row) % R
-        return member_copy(
-            own_part(owner, p),
-            own_part(owner, p),
-            grp_send.at[n_row * G + n],
-            grp_recv.at[owner * G + p],
-            n,
-        )
-
-    for n in range(1, R):
-        row_copy(n).start()
-    for n in range(1, G):
-        relay_copy(0, n).start()
-    for n_row in range(1, R):
-        owner = (r + n_row) % R
+    def part_wait(owner, member, sems, at):
         pltpu.make_async_remote_copy(
-            src_ref=own_part(owner, p),
-            dst_ref=own_part(owner, p),
+            src_ref=own_part(owner, member),
+            dst_ref=own_part(owner, member),
             send_sem=row_send.at[0],
-            recv_sem=row_recv.at[owner],
+            recv_sem=sems.at[at],
             device_id=dev(r, p),
             device_id_type=MESH,
         ).wait_recv()
-        for n in range(1, G):
-            relay_copy(n_row, n).start()
+
+    def part_copy(n_row, n, via, chips, cores):
+        owner = (r + n_row) % R
+        member = ((c + via) % C) * S + s
+        return pltpu.make_async_remote_copy(
+            src_ref=own_part(owner, member),
+            dst_ref=own_part(owner, member),
+            send_sem=grp_send.at[n_row * G + n],
+            recv_sem=grp_recv.at[owner * G + member],
+            device_id=(t_id, r, (c + chips) % C, (s + cores) % S),
+            device_id_type=MESH,
+        )
+
+    def across(n_row):
+        return [part_copy(n_row, k - 1, 0, k, 0) for k in range(1, C)]
+
+    def inside(n_row, via):
+        return [part_copy(n_row, C + via * (S - 1) + k - 2, via, 0, k) for k in range(1, S)]
+
+    for n in range(1, R):
+        row_copy(n).start()
+    for copy in across(0) + inside(0, 0):
+        copy.start()
+    for n_row in range(R):
+        owner = (r + n_row) % R
+        if n_row > 0:
+            part_wait(owner, p, row_recv, owner)
+            for copy in across(n_row) + inside(n_row, 0):
+                copy.start()
+        before = n_row - 1
+        if before >= 0:
+            owner = (r + before) % R
+            for via in range(1, C):
+                member = ((c + via) % C) * S + s
+                part_wait(owner, member, grp_recv, owner * G + member)
+                for copy in inside(before, via):
+                    copy.start()
+    last = (r + R - 1) % R
+    for via in range(1, C):
+        member = ((c + via) % C) * S + s
+        part_wait(last, member, grp_recv, last * G + member)
+        for copy in inside(R - 1, via):
+            copy.start()
 
     for n in range(1, G):
         member = (p + n) % G
@@ -399,15 +456,10 @@
     eo_ref[...] = eo_all[...].astype(F32)
 
     def grp_wait(owner):
-        for n in range(1, G):
-            member = (p + n) % G
-            member_copy(
-                own_part(owner, member),
-                own_part(owner, member),
-                grp_send.at[0],
-                grp_recv.at[owner * G + member],
-                1,
-            ).wait_recv()
+        for via in range(C):
+            for k in range(1, S):
+                member = ((c + via) % C) * S + (s + k) % S
+                part_wait(owner, member, grp_recv, owner * G + member)
 
     grp_wait(r)
     fg_ref[...] = dot(halves[0, own_rows(r), :], wc_ref[...], ((1,), (1,))) + dot(
@@ -431,8 +483,8 @@
     for copy in cnt_copies + near_copies + eo_copies:
         copy.wait_send()
     for n_row in range(R):
-        for n in range(1, G):
-            relay_copy(n_row, n).wait_send()
+        for copy in across(n_row) + [one for via in range(C) for one in inside(n_row, via)]:
+            copy.wait_send()
     for u in range(U):
         for n in range(1, G):
             far_copies[u](n).wait_send()
@@ -462,10 +514,17 @@
             out((feat, feat), F32),
             out((feat, feat), F32),
         ),
-        in_specs=[pl.BlockSpec(memory_space=pltpu.SMEM)] * 2
-        + [pl.BlockSpec(memory_space=pltpu.VMEM)] * 5,
+        in_specs=[pl.BlockSpec(memory_space=pltpu.HBM)] * 7,
         out_specs=[pl.BlockSpec(memory_space=pltpu.VMEM)] * 4,
         scratch_shapes=[
+            pltpu.SMEM((T,), jnp.int32),
+            pltpu.SMEM((T,), jnp.int32),
+            vm((points, feat), F32),
+            vm((feat, feat), BF16),
+            vm((feat, feat), BF16),
+            vm((points, feat), F32),
+            vm((T, B, B), jnp.int32),
+            dma((7,)),
             vm((R * points, feat), BF16),
             vm((2, R * points, feat), BF16),
             vm((points, feat), F32),

time: 49.3 us -> 43.7 us (0.89)
  the two profiles are of different devices: /device:TPU:0 before, /device:TPU:11 now
where the time goes in v2:
time: 43.7 us; the launch traced here: 43.5 us
  Pallas kernels  34.3 us (78%)
  local copies, waits for them, and re-layouts  8.54 us (20%)
  between operations  0.66 us (2%)
    pallas_call x1, Pallas kernels, body(): pl.pallas_call(functools.partial(kernel, sizes), out_shape=(out((points,...  34.3 us
    unnamed x18, local copies, waits for them, and re-layouts  8.54 us

profile of v2, /device:TPU:11, one launch (start us, length us, event | category | flops | bytes accessed | tf_op | source)
XLA Modules:
  0.0 43.5 jit_solution(10217079861903155324)
XLA Ops:
  0.6 0.0 copy-start
  0.6 0.9 %copy-done = f32[128,256]{1,0:T(8,128)S(1)} copy-done((f32[128,256]{1,0:T(8,128)S(1)}, f32[128,256]{1,0:T(8,128)}, u32[]{:S(2)}) %copy-start) | copy-done | bytes 131096
  1.5 0.0 copy-start.1
  1.5 0.9 %copy-done.1 = bf16[256,256]{1,0:T(8,128)(2,1)S(1)} copy-done((bf16[256,256]{1,0:T(8,128)(2,1)S(1)}, bf16[256,256]{1,0:T(8,128)(2,1)}, u32[]{:S(2)}) %copy-start.1) | copy-done | bytes 131096
  2.4 0.0 copy-start.2
  2.4 0.9 %copy-done.2 = bf16[256,256]{1,0:T(8,128)(2,1)S(1)} copy-done((bf16[256,256]{1,0:T(8,128)(2,1)S(1)}, bf16[256,256]{1,0:T(8,128)(2,1)}, u32[]{:S(2)}) %copy-start.2) | copy-done | bytes 131096
  3.3 0.0 copy-start.3
  3.4 0.9 %copy-done.3 = f32[128,256]{1,0:T(8,128)S(1)} copy-done((f32[128,256]{1,0:T(8,128)S(1)}, f32[128,256]{1,0:T(8,128)}, u32[]{:S(2)}) %copy-start.3) | copy-done | bytes 131096
  4.3 0.0 copy-start.4
  4.3 0.9 %copy-done.4 = s32[4,64,64]{2,1,0:T(8,128)S(1)} copy-done((s32[4,64,64]{2,1,0:T(8,128)S(1)}, s32[4,64,64]{2,1,0:T(8,128)}, u32[]{:S(2)}) %copy-start.4) | copy-done | bytes 65560
  5.2 0.0 copy-start.5
  5.2 0.7 %copy-done.5 = s32[4]{0:T(128)S(1)} copy-done((s32[4]{0:T(128)S(1)}, s32[4]{0:T(128)}, u32[]{:S(2)}) %copy-start.5) | copy-done | bytes 40
  5.8 0.0 copy-start.6
  5.8 0.7 %copy-done.6 = s32[4]{0:T(128)S(1)} copy-done((s32[4]{0:T(128)S(1)}, s32[4]{0:T(128)}, u32[]{:S(2)}) %copy-start.6) | copy-done | bytes 40
  6.5 34.3 %shard_map.102 = (f32[128,256]{1,0:T(8,128)S(1)}, f32[128,256]{1,0:T(8,128)S(1)}, f32[256,256]{1,0:T(8,128)S(1)}, f32[256,256]{1,0:T(8,128)S(1)}) custom-call(s32[4]{0:T(128)S(1)} %copy-done.5, s32[4]{0:T(128)S(1)} %copy-done.6, f32[128,256]{1,0:T(8,128)S(1)} %copy-done, bf16[256,256]{1,0:T(8,128)(2,1)S(1)} %copy-done.1, bf16[256,256]{1,0:T(8,128)(2,1)S(1)} %copy-done.2, ...), custom_call_target="tpu_custom_call" | custom-call | tf_op jit(solution)/shard_map/pallas_call | solution.py:509
  40.8 0.7 %copy.15 = f32[128,256]{1,0:T(8,128)} copy(f32[128,256]{1,0:T(8,128)S(1)} %get-tuple-element.8) | data formatting | bytes 262144
  41.4 0.7 %copy.16 = f32[128,256]{1,0:T(8,128)} copy(f32[128,256]{1,0:T(8,128)S(1)} %get-tuple-element.9) | data formatting | bytes 262144
  42.1 0.7 %copy.17 = f32[256,256]{1,0:T(8,128)} copy(f32[256,256]{1,0:T(8,128)S(1)} %get-tuple-element.10) | data formatting | bytes 524288
  42.8 0.7 %copy.18 = f32[256,256]{1,0:T(8,128)} copy(f32[256,256]{1,0:T(8,128)S(1)} %get-tuple-element.11) | data formatting | bytes 524288
Async XLA Ops:
  0.6 0.9 %copy-start = (f32[128,256]{1,0:T(8,128)S(1)}, f32[128,256]{1,0:T(8,128)}, u32[]{:S(2)}) copy-start(f32[128,256]{1,0:T(8,128)} %feat_h.1) | copy-start | bytes 393220
  1.5 0.9 %copy-start.1 = (bf16[256,256]{1,0:T(8,128)(2,1)S(1)}, bf16[256,256]{1,0:T(8,128)(2,1)}, u32[]{:S(2)}) copy-start(bf16[256,256]{1,0:T(8,128)(2,1)} %wc_h.1) | copy-start | bytes 393220
  2.4 0.9 %copy-start.2 = (bf16[256,256]{1,0:T(8,128)(2,1)S(1)}, bf16[256,256]{1,0:T(8,128)(2,1)}, u32[]{:S(2)}) copy-start(bf16[256,256]{1,0:T(8,128)(2,1)} %wn_h.1) | copy-start | bytes 393220
  3.3 0.9 %copy-start.3 = (f32[128,256]{1,0:T(8,128)S(1)}, f32[128,256]{1,0:T(8,128)}, u32[]{:S(2)}) copy-start(f32[128,256]{1,0:T(8,128)} %cot_h.1) | copy-start | bytes 393220
  4.3 0.9 %copy-start.4 = (s32[4,64,64]{2,1,0:T(8,128)S(1)}, s32[4,64,64]{2,1,0:T(8,128)}, u32[]{:S(2)}) copy-start(s32[4,64,64]{2,1,0:T(8,128)} %links_h.1) | copy-start | bytes 196612
  5.2 0.7 %copy-start.5 = (s32[4]{0:T(128)S(1)}, s32[4]{0:T(128)}, u32[]{:S(2)}) copy-start(s32[4]{0:T(128)} %rows_h.1) | copy-start | bytes 52
  5.8 0.7 %copy-start.6 = (s32[4]{0:T(128)S(1)}, s32[4]{0:T(128)}, u32[]{:S(2)}) copy-start(s32[4]{0:T(128)} %cols_h.1) | copy-start | bytes 52

commit v3 on v2

--- a/solution.py
+++ b/solution.py
@@ -562,7 +562,7 @@
             dma((G,)),
         ],
         compiler_params=pltpu.CompilerParams(
-            collective_id=0, has_side_effects=True, vmem_limit_bytes=48 * 1024 * 1024
+            collective_id=0, has_side_effects=True
         ),
     )(tile_rows, tile_cols, features, center_weight, neighbor_weight, cotangent, tile_links)
 

time: 43.7 us -> 39.3 us (0.90)
  local copies, waits for them, and re-layouts: 8.54 us -> 4.03 us
    unnamed x18 -> x10, local copies, waits for them, and re-layouts: 8.54 us -> 4.03 us
where the time goes in v3:
time: 39.3 us; the launch traced here: 39.1 us
  Pallas kernels  34.4 us (88%)
  local copies, waits for them, and re-layouts  4.03 us (10%)
  between operations  0.66 us (2%)
    pallas_call x1, Pallas kernels, body(): pl.pallas_call(functools.partial(kernel, sizes), out_shape=(out((points,...  34.4 us
    unnamed x10, local copies, waits for them, and re-layouts  4.03 us

profile of v3, /device:TPU:11, one launch (start us, length us, event | category | flops | bytes accessed | tf_op | source)
XLA Modules:
  0.0 39.1 jit_solution(13025170973072986371)
XLA Ops:
  0.6 34.4 %shard_map.102 = (f32[128,256]{1,0:T(8,128)}, f32[128,256]{1,0:T(8,128)}, f32[256,256]{1,0:T(8,128)}, f32[256,256]{1,0:T(8,128)}) custom-call(s32[4]{0:T(128)} %rows_h.1, s32[4]{0:T(128)} %cols_h.1, f32[128,256]{1,0:T(8,128)} %feat_h.1, bf16[256,256]{1,0:T(8,128)(2,1)} %wc_h.1, bf16[256,256]{1,0:T(8,128)(2,1)} %wn_h.1, f32[128,256]{1,0:T(8,128)} %cot_h.1, ...), custom_call_target="tpu_custom_call" | custom-call | tf_op jit(solution)/shard_map/pallas_call | solution.py:509
  35.1 0.0 copy-start.2
  35.1 0.0 copy-start.1
  35.1 1.6 %copy.15 = f32[128,256]{1,0:T(8,128)} copy(f32[128,256]{1,0:T(8,128)} %get-tuple-element.8) | data formatting | bytes 262144
  36.7 0.0 copy-done.2
  36.7 0.7 %copy.16 = f32[128,256]{1,0:T(8,128)} copy(f32[128,256]{1,0:T(8,128)S(1)} %copy-done.2) | data formatting | bytes 262144
  37.4 0.0 copy-done.1
  37.4 0.0 copy-start
  37.4 0.7 %copy.17 = f32[256,256]{1,0:T(8,128)} copy(f32[256,256]{1,0:T(8,128)S(1)} %copy-done.1) | data formatting | bytes 524288
  38.1 0.3 copy-done
  38.4 0.7 %copy.18 = f32[256,256]{1,0:T(8,128)} copy(f32[256,256]{1,0:T(8,128)S(1)} %copy-done) | data formatting | bytes 524288
Async XLA Ops:
  35.1 1.6 %copy-start.2 = (f32[128,256]{1,0:T(8,128)S(1)}, f32[128,256]{1,0:T(8,128)}, u32[]{:S(2)}) copy-start(f32[128,256]{1,0:T(8,128)} %get-tuple-element.9) | copy-start | bytes 393220
  35.1 2.3 %copy-start.1 = (f32[256,256]{1,0:T(8,128)S(1)}, f32[256,256]{1,0:T(8,128)}, u32[]{:S(2)}) copy-start(f32[256,256]{1,0:T(8,128)} %get-tuple-element.10) | copy-start | bytes 786436
  37.4 1.0 %copy-start = (f32[256,256]{1,0:T(8,128)S(1)}, f32[256,256]{1,0:T(8,128)}, u32[]{:S(2)}) copy-start(f32[256,256]{1,0:T(8,128)} %get-tuple-element.11) | copy-start | bytes 786436

commit v4 on v3

--- a/solution.py
+++ b/solution.py
@@ -110,9 +110,12 @@
 
     def greet(n, carry):
         other = (r * G + p + n) % (R * G)
-        pl.semaphore_signal(
-            barrier, inc=1, device_id=dev(other // G, other % G), device_id_type=MESH
-        )
+        row, member = other // G, other % G
+
+        @pl.when((row == r) | (member == p) | (member // S == r % C))
+        def _():
+            pl.semaphore_signal(barrier, inc=1, device_id=dev(row, member), device_id_type=MESH)
+
         return carry
 
     lax.fori_loop(1, R * G, greet, 0)
@@ -142,7 +145,8 @@
         count = [count[n] + jnp.where(jnp.full(row_sum.shape, block, jnp.int32) == n, row_sum, 0.0) for n in range(nblk)]
     cnt[pl.ds(p, 1)] = jnp.concatenate(count, axis=1)[None]
 
-    pl.semaphore_wait(barrier, R * G - 1)
+    far_rows = jnp.where(r % C == c, U - 1, U)
+    pl.semaphore_wait(barrier, R - 1 + G - 1 + far_rows * (G - 1))
 
     def fh_copy(n):
         to = (r + n) % R
@@ -287,7 +291,7 @@
                 far_acc[...] += out_d[16:]
                 return carry
 
-            lax.fori_loop(0, step, group, 0, unroll=4)
+            lax.fori_loop(0, step, group, 0, unroll=8)
             tile_e, tile_c = in_order(near_s), in_order(near_d)
             far = far_acc[...]
             for n in range(nblk):

time: 39.3 us -> 37.3 us (0.949)
  Pallas kernels: 34.4 us -> 32.4 us
    pallas_call x1, Pallas kernels: 34.4 us -> 32.4 us  [body(): pl.pallas_call(functools.partial(kernel, sizes), out_shape=(out((points,...]
where the time goes in v4:
time: 37.3 us; the launch traced here: 37.1 us
  Pallas kernels  32.4 us (87%)
  local copies, waits for them, and re-layouts  4.03 us (11%)
  between operations  0.66 us (2%)
    pallas_call x1, Pallas kernels, body(): pl.pallas_call(functools.partial(kernel, sizes), out_shape=(out((points,...  32.4 us
    unnamed x10, local copies, waits for them, and re-layouts  4.03 us

profile of v4, /device:TPU:11, one launch (start us, length us, event | category | flops | bytes accessed | tf_op | source)
XLA Modules:
  0.0 37.1 jit_solution(8231280911182249101)
XLA Ops:
  0.6 32.4 %shard_map.102 = (f32[128,256]{1,0:T(8,128)}, f32[128,256]{1,0:T(8,128)}, f32[256,256]{1,0:T(8,128)}, f32[256,256]{1,0:T(8,128)}) custom-call(s32[4]{0:T(128)} %rows_h.1, s32[4]{0:T(128)} %cols_h.1, f32[128,256]{1,0:T(8,128)} %feat_h.1, bf16[256,256]{1,0:T(8,128)(2,1)} %wc_h.1, bf16[256,256]{1,0:T(8,128)(2,1)} %wn_h.1, f32[128,256]{1,0:T(8,128)} %cot_h.1, ...), custom_call_target="tpu_custom_call" | custom-call | tf_op jit(solution)/shard_map/pallas_call | solution.py:513
  33.1 0.0 copy-start.2
  33.1 0.0 copy-start.1
  33.1 1.6 %copy.15 = f32[128,256]{1,0:T(8,128)} copy(f32[128,256]{1,0:T(8,128)} %get-tuple-element.8) | data formatting | bytes 262144
  34.7 0.0 copy-done.2
  34.7 0.7 %copy.16 = f32[128,256]{1,0:T(8,128)} copy(f32[128,256]{1,0:T(8,128)S(1)} %copy-done.2) | data formatting | bytes 262144
  35.4 0.0 copy-done.1
  35.4 0.0 copy-start
  35.4 0.7 %copy.17 = f32[256,256]{1,0:T(8,128)} copy(f32[256,256]{1,0:T(8,128)S(1)} %copy-done.1) | data formatting | bytes 524288
  36.1 0.3 copy-done
  36.4 0.7 %copy.18 = f32[256,256]{1,0:T(8,128)} copy(f32[256,256]{1,0:T(8,128)S(1)} %copy-done) | data formatting | bytes 524288
Async XLA Ops:
  33.1 1.6 %copy-start.2 = (f32[128,256]{1,0:T(8,128)S(1)}, f32[128,256]{1,0:T(8,128)}, u32[]{:S(2)}) copy-start(f32[128,256]{1,0:T(8,128)} %get-tuple-element.9) | copy-start | bytes 393220
  33.1 2.3 %copy-start.1 = (f32[256,256]{1,0:T(8,128)S(1)}, f32[256,256]{1,0:T(8,128)}, u32[]{:S(2)}) copy-start(f32[256,256]{1,0:T(8,128)} %get-tuple-element.10) | copy-start | bytes 786436
  35.4 1.0 %copy-start = (f32[256,256]{1,0:T(8,128)S(1)}, f32[256,256]{1,0:T(8,128)}, u32[]{:S(2)}) copy-start(f32[256,256]{1,0:T(8,128)} %get-tuple-element.11) | copy-start | bytes 786436

commit v5 on v4

--- a/solution.py
+++ b/solution.py
@@ -291,7 +291,7 @@
                 far_acc[...] += out_d[16:]
                 return carry
 
-            lax.fori_loop(0, step, group, 0, unroll=8)
+            lax.fori_loop(0, step, group, 0, unroll=16)
             tile_e, tile_c = in_order(near_s), in_order(near_d)
             far = far_acc[...]
             for n in range(nblk):

time: 37.3 us -> 36.2 us (0.971)
  Pallas kernels: 32.4 us -> 31.4 us
    pallas_call x1, Pallas kernels: 32.4 us -> 31.4 us  [body(): pl.pallas_call(functools.partial(kernel, sizes), out_shape=(out((points,...]
where the time goes in v5:
time: 36.2 us; the launch traced here: 36 us
  Pallas kernels  31.4 us (87%)
  local copies, waits for them, and re-layouts  4.03 us (11%)
  between operations  0.66 us (2%)
    pallas_call x1, Pallas kernels, body(): pl.pallas_call(functools.partial(kernel, sizes), out_shape=(out((points,...  31.4 us
    unnamed x10, local copies, waits for them, and re-layouts  4.03 us

profile of v5, /device:TPU:11, one launch (start us, length us, event | category | flops | bytes accessed | tf_op | source)
XLA Modules:
  0.0 36.0 jit_solution(6665725981752927976)
XLA Ops:
  0.6 31.4 %shard_map.102 = (f32[128,256]{1,0:T(8,128)}, f32[128,256]{1,0:T(8,128)}, f32[256,256]{1,0:T(8,128)}, f32[256,256]{1,0:T(8,128)}) custom-call(s32[4]{0:T(128)} %rows_h.1, s32[4]{0:T(128)} %cols_h.1, f32[128,256]{1,0:T(8,128)} %feat_h.1, bf16[256,256]{1,0:T(8,128)(2,1)} %wc_h.1, bf16[256,256]{1,0:T(8,128)(2,1)} %wn_h.1, f32[128,256]{1,0:T(8,128)} %cot_h.1, ...), custom_call_target="tpu_custom_call" | custom-call | tf_op jit(solution)/shard_map/pallas_call | solution.py:513
  32.0 0.0 copy-start.2
  32.0 0.0 copy-start.1
  32.0 1.6 %copy.15 = f32[128,256]{1,0:T(8,128)} copy(f32[128,256]{1,0:T(8,128)} %get-tuple-element.8) | data formatting | bytes 262144
  33.6 0.0 copy-done.2
  33.6 0.7 %copy.16 = f32[128,256]{1,0:T(8,128)} copy(f32[128,256]{1,0:T(8,128)S(1)} %copy-done.2) | data formatting | bytes 262144
  34.3 0.0 copy-done.1
  34.3 0.0 copy-start
  34.3 0.7 %copy.17 = f32[256,256]{1,0:T(8,128)} copy(f32[256,256]{1,0:T(8,128)S(1)} %copy-done.1) | data formatting | bytes 524288
  35.0 0.3 copy-done
  35.3 0.7 %copy.18 = f32[256,256]{1,0:T(8,128)} copy(f32[256,256]{1,0:T(8,128)S(1)} %copy-done) | data formatting | bytes 524288
Async XLA Ops:
  32.0 1.6 %copy-start.2 = (f32[128,256]{1,0:T(8,128)S(1)}, f32[128,256]{1,0:T(8,128)}, u32[]{:S(2)}) copy-start(f32[128,256]{1,0:T(8,128)} %get-tuple-element.9) | copy-start | bytes 393220
  32.0 2.3 %copy-start.1 = (f32[256,256]{1,0:T(8,128)S(1)}, f32[256,256]{1,0:T(8,128)}, u32[]{:S(2)}) copy-start(f32[256,256]{1,0:T(8,128)} %get-tuple-element.10) | copy-start | bytes 786436
  34.3 1.0 %copy-start = (f32[256,256]{1,0:T(8,128)S(1)}, f32[256,256]{1,0:T(8,128)}, u32[]{:S(2)}) copy-start(f32[256,256]{1,0:T(8,128)} %get-tuple-element.11) | copy-start | bytes 786436
